TPU v7x, 32 devices: a whole 2x2x4 slice. The times are simulated.
32 devices in a mesh: tx: 8 (over y, x, core), ty: 4 (over z).
Axes of the slice: x: 2, y: 2, z: 4, core: 2. Of those that a mesh axis runs over, the one named last changes fastest.
Arguments:
- adjoint_in: float32 [5, 3, 64, 64, 128], P(None, None, 'ty', 'tx'), may hold values from -6 to 6
- courant: float32 [2, 3, 64, 64, 128], P(None, None, 'ty', 'tx'), may hold values from -0.45 to 0.45
- vertical_inverse: float32 [5, 128, 128], replicated, as said below
- links: int32 [40, 4], replicated, may hold values from 0 to 95, as said below
Outputs:
- adjoint_out: float32 [5, 3, 64, 64, 128], P(None, None, 'ty', 'tx')
Inputs may be any that keep to these rules, and one draw needn't show every extreme that they name: `links`: the three panel slots hold three faces of a cube that meet at one corner, in an order drawn afresh; call them X, Y, Z. X's east side joins Y's west side (code 0, both ways, tile row to same tile row), X's north side joins Z's south side (code 1, both ways, tile column to same tile column), Y's north side joins Z's east side with rotation: cell x = i of Y's top row is the neighbour of cell y = i of Z's east column (code 2 for Z's east ghosts, two rows a tile with off 0 and 8; code 3 for Y's north ghosts, one row a tile with off 0 or 8); all other panel sides are open. Row order is drawn afresh. Offsets are 0 or 8, codes 0 to 3. `vertical_inverse`: each block has a diagonal in [0.6, 1.0) and independent off-diagonal entries.
All inputs are finite; a program needn't handle non-finite values.
Results may differ from a plain program's by a relative error of at most 0.0003.
Values sent between devices are 32-bit elements; how exact they have to be, the bound alone decides.
A program may use at most 64 MiB of HBM per device.

v0:
```python
import jax
import jax.numpy as jnp
from jax import lax
from jax.sharding import PartitionSpec as P

STEPS = 2


def with_halo(block, sides, width):
    for axis, dim in sides:
        count = lax.axis_size(axis)
        forward = [(i, i + 1) for i in range(count - 1)]
        forward.append((count - 1, 0))
        backward = [(target, source) for source, target in forward]
        low = lax.ppermute(
            lax.slice_in_dim(block, block.shape[dim] - width, None, axis=dim), axis, forward
        )
        high = lax.ppermute(lax.slice_in_dim(block, 0, width, axis=dim), axis, backward)
        block = jnp.concatenate([low, block, high], axis=dim)
    return block


def broadcast(block, axis, source):
    block = jnp.where(lax.axis_index(axis) == source, block, jnp.zeros_like(block))
    return lax.psum(block, axis)


def link_tables(links, own_tile, tile_count, slot_count):
    source_slot = links[:, 0] // tile_count
    target_slot = links[:, 1] // tile_count
    target_tile = links[:, 1] % tile_count
    offset = links[:, 2]
    link_kind = links[:, 3]
    slot_ids = jnp.arange(slot_count, dtype=jnp.int32)
    target_hot = (target_slot[:, None] == slot_ids[None, :]).astype(jnp.float32)
    source_hot = (source_slot[:, None] == slot_ids[None, :]).astype(jnp.float32)

    def slot_table(wanted):
        chosen = (
            (target_tile == own_tile) & (link_kind == wanted) & ((link_kind != 2) | (offset == 0))
        )
        weight = chosen.astype(jnp.float32)
        return jnp.sum(
            weight[:, None, None] * target_hot[:, :, None] * source_hot[:, None, :], axis=0
        )

    north_source = jnp.max(jnp.where(link_kind == 2, source_slot, 0))
    east_source = jnp.max(jnp.where(link_kind == 3, source_slot, 0))
    return (slot_table(0), slot_table(1), slot_table(2), slot_table(3), north_source, east_source)


def mix_slots(slot_table, pieces):
    return jnp.sum(slot_table[None, :, :, None, None] * pieces[:, None], axis=2)


def on_device(adjoint_in, courant, vertical_inverse, links):
    col_count = lax.axis_size("tx")
    row_count = lax.axis_size("ty")
    column = lax.axis_index("tx")
    row_index = lax.axis_index("ty")
    slot_count = adjoint_in.shape[1]
    cells_y = adjoint_in.shape[2]
    cells_x = adjoint_in.shape[3]
    tile_count = col_count * row_count
    own_tile = row_index * col_count + column
    x_table, y_table, east_table, north_table, north_source, east_source = link_tables(
        links, own_tile, tile_count, slot_count
    )
    at_east = column == col_count - 1
    at_west = column == 0
    at_north = row_index == row_count - 1
    at_south = row_index == 0
    adjoint = adjoint_in
    for step_index in range(STEPS):
        mixed = jnp.einsum(
            "slm,skyxl->skyxm", vertical_inverse, adjoint, precision=lax.Precision.HIGHEST
        )
        fluxes = courant[:, None] * mixed[None]
        padded = with_halo(fluxes, (("tx", 4), ("ty", 3)), 1)
        halo_east = padded[0, :, :, 1:-1, cells_x + 1]
        halo_west = padded[0, :, :, 1:-1, 0]
        halo_north = padded[1, :, :, cells_y + 1, 1:-1]
        halo_south = padded[1, :, :, 0, 1:-1]
        top_rows = lax.dynamic_slice_in_dim(fluxes[1, :, :, cells_y - 1], north_source, 1, 1)
        east_cols = lax.dynamic_slice_in_dim(fluxes[0, :, :, :, cells_x - 1], east_source, 1, 1)
        north_below = broadcast(top_rows, "ty", row_count - 1)
        north_whole = lax.all_gather(north_below, "tx", axis=2, tiled=True)
        east_beside = broadcast(east_cols, "tx", col_count - 1)
        east_whole = lax.all_gather(east_beside, "ty", axis=2, tiled=True)
        north_piece = lax.dynamic_slice_in_dim(north_whole, row_index * cells_y, cells_y, 2)
        east_piece = lax.dynamic_slice_in_dim(east_whole, column * cells_x, cells_x, 2)
        rotated_east = -jnp.sum(east_table, axis=1)[None, :, None, None] * north_piece
        rotated_north = -jnp.sum(north_table, axis=1)[None, :, None, None] * east_piece
        ghost_east = jnp.where(at_east, mix_slots(x_table, halo_east) + rotated_east, halo_east)
        ghost_west = jnp.where(at_west, mix_slots(x_table, halo_west), halo_west)
        ghost_north = jnp.where(
            at_north, mix_slots(y_table, halo_north) + rotated_north, halo_north
        )
        ghost_south = jnp.where(at_south, mix_slots(y_table, halo_south), halo_south)
        x_line = jnp.concatenate(
            [ghost_west[:, :, :, None], fluxes[0], ghost_east[:, :, :, None]], axis=3
        )
        y_line = jnp.concatenate(
            [ghost_south[:, :, None], fluxes[1], ghost_north[:, :, None]], axis=2
        )
        adjoint = (
            mixed
            + 0.5 * (x_line[:, :, :, 2:] - x_line[:, :, :, :-2])
            + 0.5 * (y_line[:, :, 2:] - y_line[:, :, :-2])
        )
    return adjoint


def solution(mesh):
    placed = (P(None, None, "ty", "tx", None), P(None, None, "ty", "tx", None), P(), P())
    return jax.shard_map(
        on_device,
        mesh=mesh,
        in_specs=placed,
        out_specs=P(None, None, "ty", "tx", None),
        check_vma=False,
    )
```

profile of v0, /device:TPU:0, one launch (start us, length us, event | category | flops | bytes accessed | tf_op | source)
XLA Modules:
  0.0 178.6 jit_solution(6658720027340490278)
XLA Ops:
  0.0 1.2 copy.186
  1.2 0.2 copy-done
  1.3 1.9 %fusion.13 = f32[5,3,16,8,128]{4,3,2,1,0:T(8,128)S(1)} fusion(f32[5,3,16,8,128]{4,3,2,1,0:T(8,128)S(1)} %copy-done, f32[5,128,128]{2,1,0:T(8,128)} %param.6), kind=kOutput, calls=%fused_computation.33 | convolution fusion | flops 377487360 | bytes 2293760 | tf_op jit(solution)/shard_map/slm,skyxl->skyxm/dot_general | solution.py:75
  3.3 0.9 copy-done.1
  4.2 0.2 copy.187
  4.4 0.2 broadcast_multiply_fusion.1
  4.6 0.8 fusion.36
  5.4 0.5 collective-permute-start.1
  5.9 2.9 %collective-permute-start = (f32[2,5,3,16,1,128]{5,3,2,1,4,0:T(8,128)}, f32[2,5,3,16,1,128]{5,3,2,1,4,0:T(8,128)}, u32[]{:S(2)}, u32[]{:S(2)}) collective-permute-start(f32[2,5,3,16,1,128]{5,3,2,1,4,0:T(8,128)} %get-tuple-element.33), channel_id=1, source_target_pairs={{4,0},{8,4},{12,8},{16,12},{20,16},{24,20},{28,24},{0,28},{5,1},{9... | collective-permute-start | bytes 737288 | tf_op jit(solution)/shard_map/ppermute | solution.py:18
  8.8 0.7 fusion.28
  12.5 0.6 neg.18
  13.1 0.5 neg.19
  14.3 20.5 %psum.28 = f32[5,1,8,128]{3,2,0,1:T(8,128)} all-reduce(f32[5,1,8,128]{3,2,0,1:T(8,128)S(1)} %bitcast.157), channel_id=1, replica_groups=mesh['tx'=8,'ty'=4] {'ty'}, use_global_device_ids=true, to_apply=%region_4.5 | all-reduce | flops 5120 | bytes 40960 | tf_op jit(solution)/shard_map/psum | solution.py:25
  35.5 22.7 %psum.29 = f32[5,1,16,128]{3,2,0,1:T(8,128)S(1)} all-reduce(f32[5,1,16,128]{3,2,0,1:T(8,128)S(1)} %select_bitcast_fusion.1), channel_id=1, replica_groups=mesh['tx'=8,'ty'=4] {'tx'}, use_global_device_ids=true, to_apply=%region_10.11 | all-reduce | flops 10240 | bytes 81920 | tf_op jit(solution)/shard_map/psum | solution.py:25
  58.3 13.5 %all_gather.13 = f32[5,1,64,128]{3,2,0,1:T(8,128)S(1)} all-gather(f32[5,1,16,128]{3,2,0,1:T(8,128)S(1)} %psum.29), channel_id=1, replica_groups=mesh['tx'=8,'ty'=4] {'ty'}, dimensions={2}, use_global_device_ids=true | all-gather | bytes 204800 | tf_op jit(solution)/shard_map/all_gather | solution.py:89
  71.7 9.5 %all_gather.12 = f32[5,1,64,128]{3,2,0,1:T(8,128)S(1)} all-gather(f32[5,1,8,128]{3,2,0,1:T(8,128)} %psum.28), channel_id=1, replica_groups=mesh['tx'=8,'ty'=4] {'tx'}, dimensions={2}, use_global_device_ids=true | all-gather | bytes 184320 | tf_op jit(solution)/shard_map/all_gather | solution.py:87
  81.2 0.1 slice_bitcast_fusion.2
  81.4 1.3 pad_maximum_fusion.13
  82.7 0.1 collective-permute-start.2
  82.8 1.9 %collective-permute-start.3 = (f32[2,5,3,1,10,128]{5,3,2,1,4,0:T(1,128)S(1)}, f32[2,5,3,1,10,128]{5,3,2,1,4,0:T(1,128)S(1)}, u32[]{:S(2)}, u32[]{:S(2)}) collective-permute-start(f32[2,5,3,1,10,128]{5,3,2,1,4,0:T(1,128)S(1)} %get-tuple-element.25), channel_id=1, source_target_pairs={{0,1},{1,2},{2,3},{3,0},{4,5},{5,6},{6,7},{7,4},{8,9},{9,10},{10,1... | collective-permute-start | bytes 460808 | tf_op jit(solution)/shard_map/ppermute | solution.py:15
  84.8 0.9 slice_bitcast_fusion.4
  85.7 0.9 slice_bitcast_fusion.5
  86.7 1.0 bitcast_select_fusion.2
  87.7 0.9 bitcast_select_fusion.1
  88.8 0.7 collective-permute-done.2
  89.5 2.8 %collective-permute-done.3 = f32[2,5,3,1,10,128]{5,3,2,1,4,0:T(1,128)S(1)} collective-permute-done((f32[2,5,3,1,10,128]{5,3,2,1,4,0:T(1,128)S(1)}, f32[2,5,3,1,10,128]{5,3,2,1,4,0:T(1,128)S(1)}, u32[]{:S(2)}, u32[]{:S(2)}) %collective-permute-start.3) | collective-permute-done | bytes 153632 | tf_op jit(solution)/shard_map/ppermute | solution.py:15
  92.6 0.2 broadcast_select_fusion.4
  92.7 0.3 fusion.5
  93.0 1.7 fusion.9
  94.8 0.2 copy.201
  95.0 0.2 broadcast_multiply_fusion
  95.1 0.6 copy-done.3
  95.8 0.8 fusion.35
  96.6 1.4 slice_bitcast_fusion
  98.1 23.2 %psum.31 = f32[5,1,16,128]{3,2,0,1:T(8,128)S(1)} all-reduce(f32[5,1,16,128]{3,2,0,1:T(8,128)S(1)} %select_bitcast_fusion), channel_id=1, replica_groups=mesh['tx'=8,'ty'=4] {'tx'}, use_global_device_ids=true, to_apply=%region_16.17 | all-reduce | flops 10240 | bytes 81920 | tf_op jit(solution)/shard_map/psum | solution.py:25
  121.3 13.4 %all_gather.15 = f32[5,1,64,128]{3,2,0,1:T(8,128)S(1)} all-gather(f32[5,1,16,128]{3,2,0,1:T(8,128)S(1)} %psum.31), channel_id=1, replica_groups=mesh['tx'=8,'ty'=4] {'ty'}, dimensions={2}, use_global_device_ids=true | all-gather | bytes 204800 | tf_op jit(solution)/shard_map/all_gather | solution.py:89
  134.7 2.6 %collective-permute-start.4 = (f32[2,5,3,16,1,128]{5,3,2,1,4,0:T(8,128)}, f32[2,5,3,16,1,128]{5,3,2,1,4,0:T(8,128)S(1)}, u32[]{:S(2)}, u32[]{:S(2)}) collective-permute-start(f32[2,5,3,16,1,128]{5,3,2,1,4,0:T(8,128)} %get-tuple-element.29), channel_id=1, source_target_pairs={{4,0},{8,4},{12,8},{16,12},{20,16},{24,20},{28,24},{0,28},{5,1},{9... | collective-permute-start | bytes 737288 | tf_op jit(solution)/shard_map/ppermute | solution.py:18
  137.4 2.5 %copy.252 = f32[1,5,3,16,8,128]{5,4,3,2,1,0:T(8,128)} copy(f32[1,5,3,16,8,128]{5,3,2,1,4,0:T(8,128)} %get-tuple-element.27) | data formatting | bytes 1966080 | tf_op jit(solution)/shard_map/slice | solution.py:101
  139.9 17.6 %psum.30 = f32[5,1,8,128]{3,2,0,1:T(8,128)S(1)} all-reduce(f32[5,1,8,128]{3,2,0,1:T(8,128)S(1)} %bitcast.156), channel_id=1, replica_groups=mesh['tx'=8,'ty'=4] {'ty'}, use_global_device_ids=true, to_apply=%region_13.14 | all-reduce | flops 5120 | bytes 40960 | tf_op jit(solution)/shard_map/psum | solution.py:25
  157.5 8.7 %all_gather.14 = f32[5,1,64,128]{3,2,0,1:T(8,128)S(1)} all-gather(f32[5,1,8,128]{3,2,0,1:T(8,128)S(1)} %psum.30), channel_id=1, replica_groups=mesh['tx'=8,'ty'=4] {'tx'}, dimensions={2}, use_global_device_ids=true | all-gather | bytes 184320 | tf_op jit(solution)/shard_map/all_gather | solution.py:87
  166.2 0.2 pad_maximum_fusion.10
  166.5 2.0 %collective-permute-start.7 = (f32[2,5,3,1,10,128]{5,3,2,1,4,0:T(1,128)S(1)}, f32[2,5,3,1,10,128]{5,3,2,1,4,0:T(1,128)S(1)}, u32[]{:S(2)}, u32[]{:S(2)}) collective-permute-start(f32[2,5,3,1,10,128]{5,3,2,1,4,0:T(1,128)S(1)} %get-tuple-element.23), channel_id=1, source_target_pairs={{0,1},{1,2},{2,3},{3,0},{4,5},{5,6},{6,7},{7,4},{8,9},{9,10},{10,1... | collective-permute-start | bytes 460808 | tf_op jit(solution)/shard_map/ppermute | solution.py:15
  168.6 0.1 multiply_reduce_fusion.1
  168.8 4.4 %collective-permute-done.6 = f32[2,5,3,1,10,128]{5,3,2,1,4,0:T(1,128)S(1)} collective-permute-done((f32[2,5,3,1,10,128]{5,3,2,1,4,0:T(1,128)S(1)}, f32[2,5,3,1,10,128]{5,3,2,1,4,0:T(1,128)S(1)}, u32[]{:S(2)}, u32[]{:S(2)}) %collective-permute-start.6) | collective-permute-done | bytes 153632 | tf_op jit(solution)/shard_map/ppermute | solution.py:18
  173.3 2.8 %collective-permute-done.7 = f32[2,5,3,1,10,128]{5,3,2,1,4,0:T(1,128)S(1)} collective-permute-done((f32[2,5,3,1,10,128]{5,3,2,1,4,0:T(1,128)S(1)}, f32[2,5,3,1,10,128]{5,3,2,1,4,0:T(1,128)S(1)}, u32[]{:S(2)}, u32[]{:S(2)}) %collective-permute-start.7) | collective-permute-done | bytes 153632 | tf_op jit(solution)/shard_map/ppermute | solution.py:15
  176.3 0.2 broadcast_select_fusion.3
  176.5 0.3 fusion
  176.8 1.8 fusion.4
  (66 shorter events, 1.4 us)
Async XLA Ops:
  0.0 1.3 copy-start
  3.3 0.9 copy-start.1
  4.4 4.3 %copy-start.8 = (s32[40,4]{0,1:T(4,128)S(1)}, s32[40,4]{0,1:T(4,128)}, u32[]{:S(2)}) copy-start(s32[40,4]{0,1:T(4,128)} %param.7) | copy-start | bytes 1924
  5.4 75.9 %collective-permute-start.1 = (f32[2,5,3,16,1,128]{5,3,2,1,4,0:T(8,128)}, f32[2,5,3,16,1,128]{5,3,2,1,4,0:T(8,128)}, u32[]{:S(2)}, u32[]{:S(2)}) collective-permute-start(f32[2,5,3,16,1,128]{5,3,2,1,4,0:T(8,128)} %get-tuple-element.32), channel_id=1, source_target_pairs={{0,4},{4,8},{8,12},{12,16},{16,20},{20,24},{24,28},{28,0},{1,5},{5... | collective-permute-start | bytes 737288 | tf_op jit(solution)/shard_map/ppermute | solution.py:15
  5.9 75.5 %collective-permute-start = (f32[2,5,3,16,1,128]{5,3,2,1,4,0:T(8,128)}, f32[2,5,3,16,1,128]{5,3,2,1,4,0:T(8,128)}, u32[]{:S(2)}, u32[]{:S(2)}) collective-permute-start(f32[2,5,3,16,1,128]{5,3,2,1,4,0:T(8,128)} %get-tuple-element.33), channel_id=1, source_target_pairs={{4,0},{8,4},{12,8},{16,12},{20,16},{24,20},{28,24},{0,28},{5,1},{9... | collective-permute-start | bytes 737288 | tf_op jit(solution)/shard_map/ppermute | solution.py:18
  81.3 5.4 %copy-start.10 = (f32[3]{0:T(128)S(1)}, f32[3]{0:T(128)}, u32[]{:S(2)}) copy-start(f32[3]{0:T(128)} %neg.18) | copy-start | bytes 40
  82.7 6.8 %collective-permute-start.2 = (f32[2,5,3,1,10,128]{5,3,2,1,4,0:T(1,128)S(1)}, f32[2,5,3,1,10,128]{5,3,2,1,4,0:T(1,128)S(1)}, u32[]{:S(2)}, u32[]{:S(2)}) collective-permute-start(f32[2,5,3,1,10,128]{5,3,2,1,4,0:T(1,128)S(1)} %get-tuple-element.24), channel_id=1, source_target_pairs={{1,0},{2,1},{3,2},{0,3},{5,4},{6,5},{7,6},{4,7},{9,8},{10,9},{11,1... | collective-permute-start | bytes 460808 | tf_op jit(solution)/shard_map/ppermute | solution.py:18
  82.8 9.5 %collective-permute-start.3 = (f32[2,5,3,1,10,128]{5,3,2,1,4,0:T(1,128)S(1)}, f32[2,5,3,1,10,128]{5,3,2,1,4,0:T(1,128)S(1)}, u32[]{:S(2)}, u32[]{:S(2)}) collective-permute-start(f32[2,5,3,1,10,128]{5,3,2,1,4,0:T(1,128)S(1)} %get-tuple-element.25), channel_id=1, source_target_pairs={{0,1},{1,2},{2,3},{3,0},{4,5},{5,6},{6,7},{7,4},{8,9},{9,10},{10,1... | collective-permute-start | bytes 460808 | tf_op jit(solution)/shard_map/ppermute | solution.py:15
  86.7 5.9 %copy-start.9 = (f32[3]{0:T(128)S(1)}, f32[3]{0:T(128)}, u32[]{:S(2)}) copy-start(f32[3]{0:T(128)} %neg.19) | copy-start | bytes 40
  88.7 4.3 %copy-start.2 = (f32[5,3,16,8,128]{4,3,2,1,0:T(8,128)S(1)}, f32[5,3,16,8,128]{4,3,2,1,0:T(8,128)}, u32[]{:S(2)}) copy-start(f32[5,3,16,8,128]{4,3,2,1,0:T(8,128)} %copy-done.1) | copy-start | bytes 2949124
  88.8 4.3 %copy-start.7 = (f32[5,128,128]{2,1,0:T(8,128)S(1)}, f32[5,128,128]{2,1,0:T(8,128)}, u32[]{:S(2)}) copy-start(f32[5,128,128]{2,1,0:T(8,128)} %param.6) | copy-start | bytes 983044
  94.8 0.9 copy-start.3
  134.7 31.5 %collective-permute-start.5 = (f32[2,5,3,16,1,128]{5,3,2,1,4,0:T(8,128)}, f32[2,5,3,16,1,128]{5,3,2,1,4,0:T(8,128)S(1)}, u32[]{:S(2)}, u32[]{:S(2)}) collective-permute-start(f32[2,5,3,16,1,128]{5,3,2,1,4,0:T(8,128)} %get-tuple-element.28), channel_id=1, source_target_pairs={{0,4},{4,8},{8,12},{12,16},{16,20},{20,24},{24,28},{28,0},{1,5},{5... | collective-permute-start | bytes 737288 | tf_op jit(solution)/shard_map/ppermute | solution.py:15
  134.7 31.5 %collective-permute-start.4 = (f32[2,5,3,16,1,128]{5,3,2,1,4,0:T(8,128)}, f32[2,5,3,16,1,128]{5,3,2,1,4,0:T(8,128)S(1)}, u32[]{:S(2)}, u32[]{:S(2)}) collective-permute-start(f32[2,5,3,16,1,128]{5,3,2,1,4,0:T(8,128)} %get-tuple-element.29), channel_id=1, source_target_pairs={{4,0},{8,4},{12,8},{16,12},{20,16},{24,20},{28,24},{0,28},{5,1},{9... | collective-permute-start | bytes 737288 | tf_op jit(solution)/shard_map/ppermute | solution.py:18
  166.4 10.1 %copy-start.5 = (f32[5,3,16,8,128]{4,2,1,0,3:T(8,128)S(1)}, f32[5,3,16,8,128]{4,2,1,0,3:T(8,128)}, u32[]{:S(2)}) copy-start(f32[5,3,16,8,128]{4,2,1,0,3:T(8,128)} %get-tuple-element.26) | copy-start | bytes 2949124
  166.4 6.8 %collective-permute-start.6 = (f32[2,5,3,1,10,128]{5,3,2,1,4,0:T(1,128)S(1)}, f32[2,5,3,1,10,128]{5,3,2,1,4,0:T(1,128)S(1)}, u32[]{:S(2)}, u32[]{:S(2)}) collective-permute-start(f32[2,5,3,1,10,128]{5,3,2,1,4,0:T(1,128)S(1)} %get-tuple-element.22), channel_id=1, source_target_pairs={{1,0},{2,1},{3,2},{0,3},{5,4},{6,5},{7,6},{4,7},{9,8},{10,9},{11,1... | collective-permute-start | bytes 460808 | tf_op jit(solution)/shard_map/ppermute | solution.py:18
  166.5 9.6 %collective-permute-start.7 = (f32[2,5,3,1,10,128]{5,3,2,1,4,0:T(1,128)S(1)}, f32[2,5,3,1,10,128]{5,3,2,1,4,0:T(1,128)S(1)}, u32[]{:S(2)}, u32[]{:S(2)}) collective-permute-start(f32[2,5,3,1,10,128]{5,3,2,1,4,0:T(1,128)S(1)} %get-tuple-element.23), channel_id=1, source_target_pairs={{0,1},{1,2},{2,3},{3,0},{4,5},{5,6},{6,7},{7,4},{8,9},{9,10},{10,1... | collective-permute-start | bytes 460808 | tf_op jit(solution)/shard_map/ppermute | solution.py:15
  168.8 8.0 %copy-start.4 = (f32[5,3,16,8,128]{4,3,2,1,0:T(8,128)S(1)}, f32[5,3,16,8,128]{4,3,2,1,0:T(8,128)}, u32[]{:S(2)}) copy-start(f32[5,3,16,8,128]{4,3,2,1,0:T(8,128)} %copy-done.3) | copy-start | bytes 2949124
  168.8 8.0 %copy-start.6 = (f32[1,5,3,16,8,128]{5,4,3,2,1,0:T(8,128)S(1)}, f32[1,5,3,16,8,128]{5,4,3,2,1,0:T(8,128)}, u32[]{:S(2)}) copy-start(f32[1,5,3,16,8,128]{5,4,3,2,1,0:T(8,128)} %copy.252) | copy-start | bytes 2949124
where the time goes:
time: 179 us
  blocking collectives  129 us (72%)
  local copies, waits for them, and re-layouts  11.1 us (6%)
  waiting for transfers between devices  10.7 us (6%)
  starting transfers between devices  10.1 us (6%)
  other arithmetic  9.29 us (5%)
  between operations  4.59 us (3%)
  matrix products  3.63 us (2%)
    psum x4, blocking collectives, broadcast(): return lax.psum(block, axis)  84 us
    all_gather x2, blocking collectives, on_device(): east_whole = lax.all_gather(east_beside, 'ty', axis=2, tiled=True)  26.9 us
    all_gather x2, blocking collectives, on_device(): north_whole = lax.all_gather(north_below, 'tx', axis=2, tiled=True)  18.2 us
    ppermute x4, starting transfers between devices, with_halo(): lax.ppermute(lax.slice_in_dim(block, 0, width, axis=dim), axis, backward)  5.73 us
    ppermute x4, waiting for transfers between devices, with_halo(): lax.ppermute(lax.slice_in_dim(block, block.shape[dim] - width, None, axis...  5.56 us
    ppermute x4, waiting for transfers between devices, with_halo(): lax.ppermute(lax.slice_in_dim(block, 0, width, axis=dim), axis, backward)  5.12 us
    ppermute x4, starting transfers between devices, with_halo(): lax.ppermute(lax.slice_in_dim(block, block.shape[dim] - width, None, axis...  4.4 us
    dot_general x2, matrix products, on_device(): jnp.einsum('slm,skyxl->skyxm', vertical_inverse, adjoint, precision=lax.P...  3.63 us
  transfers between devices with their start and end apart: 8, of which 4 were waited for; matrix products, arithmetic and copies ran while one was open for 5% of the time, Pallas kernels for 0%

commit v1 on v0

--- a/solution.py
+++ b/solution.py
@@ -86,7 +86,15 @@
         north_below = broadcast(top_rows, "ty", row_count - 1)
         north_whole = lax.all_gather(north_below, "tx", axis=2, tiled=True)
         east_beside = broadcast(east_cols, "tx", col_count - 1)
-        east_whole = lax.all_gather(east_beside, "ty", axis=2, tiled=True)
+        ways, here = (lax.axis_size("ty"), lax.axis_index("ty"))
+        grown, reach = (east_beside, 1)
+        while reach < ways:
+            theirs = lax.ppermute(grown, "ty", [(d, d ^ reach) for d in range(ways)])
+            mine_first = jnp.concatenate([grown, theirs], axis=2)
+            theirs_first = jnp.concatenate([theirs, grown], axis=2)
+            grown = jnp.where(here & reach == 0, mine_first, theirs_first)
+            reach = 2 * reach
+        east_whole = grown
         north_piece = lax.dynamic_slice_in_dim(north_whole, row_index * cells_y, cells_y, 2)
         east_piece = lax.dynamic_slice_in_dim(east_whole, column * cells_x, cells_x, 2)
         rotated_east = -jnp.sum(east_table, axis=1)[None, :, None, None] * north_piece

time: 179 us -> 170 us (0.950)
  blocking collectives: 129 us -> 102 us
  waiting for transfers between devices: 10.7 us -> 18.1 us
  other arithmetic: 9.29 us -> 15.1 us
  starting transfers between devices: 10.1 us -> 13.1 us
    all_gather x2 -> x0, blocking collectives: 26.9 us -> none  [on_device(): east_whole = lax.all_gather(east_beside, 'ty', axis=2, tiled=True)]
    ppermute x0 -> x4, waiting for transfers between devices: none -> 8.67 us  [on_device(): theirs = lax.ppermute(grown, 'ty', [(d, d ^ reach) for d in range(ways)])]
    ppermute x0 -> x4, starting transfers between devices: none -> 3.1 us  [on_device(): theirs = lax.ppermute(grown, 'ty', [(d, d ^ reach) for d in range(ways)])]
    ppermute x4, starting transfers between devices: 4.4 us -> 2.42 us  [with_halo(): lax.ppermute(lax.slice_in_dim(block, block.shape[dim] - width, None, axis...]
    ppermute x4, starting transfers between devices: 5.73 us -> 7.61 us  [with_halo(): lax.ppermute(lax.slice_in_dim(block, 0, width, axis=dim), axis, backward)]
    unnamed x23 -> x33, local copies, waits for them, and re-layouts: 2.87 us -> 4.02 us
  transfers between devices with their start and end apart: 8 -> 12, of which waited for: 4 -> 6; matrix products, arithmetic and copies ran while one was open for 5% -> 8% of each run, Pallas kernels for 0% -> 0%
where the time goes in v1:
time: 170 us; the launch traced here: 169 us
  blocking collectives  102 us (60%)
  waiting for transfers between devices  18.1 us (11%)
  other arithmetic  15.1 us (9%)
  starting transfers between devices  13.1 us (8%)
  local copies, waits for them, and re-layouts  12.3 us (7%)
  between operations  4.46 us (3%)
  matrix products  3.64 us (2%)
    psum x4, blocking collectives, broadcast(): return lax.psum(block, axis)  84.6 us
    all_gather x2, blocking collectives, on_device(): north_whole = lax.all_gather(north_below, 'tx', axis=2, tiled=True)  17.9 us
    ppermute x4, waiting for transfers between devices, on_device(): theirs = lax.ppermute(grown, 'ty', [(d, d ^ reach) for d in range(ways)])  8.67 us
    ppermute x4, starting transfers between devices, with_halo(): lax.ppermute(lax.slice_in_dim(block, 0, width, axis=dim), axis, backward)  7.61 us
    ppermute x4, waiting for transfers between devices, with_halo(): lax.ppermute(lax.slice_in_dim(block, block.shape[dim] - width, None, axis...  5.67 us
    unnamed x33, local copies, waits for them, and re-layouts  4.02 us
    ppermute x4, waiting for transfers between devices, with_halo(): lax.ppermute(lax.slice_in_dim(block, 0, width, axis=dim), axis, backward)  3.72 us
    dot_general x2, matrix products, on_device(): jnp.einsum('slm,skyxl->skyxm', vertical_inverse, adjoint, precision=lax.P...  3.64 us
  transfers between devices with their start and end apart: 12, of which 6 were waited for; matrix products, arithmetic and copies ran while one was open for 8% of the time, Pallas kernels for 0%

profile of v1, /device:TPU:0, one launch (start us, length us, event | category | flops | bytes accessed | tf_op | source)
XLA Modules:
  0.0 169.1 jit_solution(7063128167973631640)
XLA Ops:
  0.0 1.4 fusion.41
  2.8 1.1 copy.247
  3.8 1.9 %fusion.13 = f32[5,3,16,8,128]{4,3,2,1,0:T(8,128)S(1)} fusion(f32[5,3,16,8,128]{4,3,2,1,0:T(8,128)S(1)} %copy-done, f32[5,128,128]{2,1,0:T(8,128)} %param.6), kind=kOutput, calls=%fused_computation.33 | convolution fusion | flops 377487360 | bytes 2293760 | tf_op jit(solution)/shard_map/slm,skyxl->skyxm/dot_general | solution.py:75
  5.8 0.9 copy-done.1
  7.8 25.9 %psum.29 = f32[5,1,16,128]{3,2,0,1:T(8,128)S(1)} all-reduce(f32[5,1,16,128]{3,2,0,1:T(8,128)S(1)} %select_bitcast_fusion), channel_id=1, replica_groups=mesh['tx'=8,'ty'=4] {'tx'}, use_global_device_ids=true, to_apply=%region_10.11 | all-reduce | flops 10240 | bytes 81920 | tf_op jit(solution)/shard_map/psum | solution.py:25
  33.7 1.6 collective-permute-start.3
  35.3 0.8 fusion.49
  36.1 2.6 %collective-permute-start = (f32[2,5,3,16,1,128]{5,3,1,4,2,0:T(8,128)}, f32[2,5,3,16,1,128]{5,3,1,4,2,0:T(8,128)}, u32[]{:S(2)}, u32[]{:S(2)}) collective-permute-start(f32[2,5,3,16,1,128]{5,3,1,4,2,0:T(8,128)} %get-tuple-element.33), channel_id=1, source_target_pairs={{4,0},{8,4},{12,8},{16,12},{20,16},{24,20},{28,24},{0,28},{5,1},{9... | collective-permute-start | bytes 737288 | tf_op jit(solution)/shard_map/ppermute | solution.py:18
  38.8 0.6 fusion.44
  40.7 1.5 slice_bitcast_fusion.2
  42.2 0.6 fusion.39
  43.4 18.6 %psum.28 = f32[5,1,8,128]{3,2,0,1:T(8,128)} all-reduce(f32[5,1,8,128]{3,2,0,1:T(8,128)S(1)} %bitcast.179), channel_id=1, replica_groups=mesh['tx'=8,'ty'=4] {'ty'}, use_global_device_ids=true, to_apply=%region_4.5 | all-reduce | flops 5120 | bytes 40960 | tf_op jit(solution)/shard_map/psum | solution.py:25
  62.1 8.5 %all_gather.6 = f32[5,1,64,128]{3,2,0,1:T(8,128)S(1)} all-gather(f32[5,1,8,128]{3,2,0,1:T(8,128)} %psum.28), channel_id=1, replica_groups=mesh['tx'=8,'ty'=4] {'tx'}, dimensions={2}, use_global_device_ids=true | all-gather | bytes 184320 | tf_op jit(solution)/shard_map/all_gather | solution.py:87
  70.6 0.7 fusion.34
  71.2 0.6 dynamic-slice_bitcast_fusion.1
  71.8 0.7 fusion.31
  72.6 0.8 copy.299
  73.5 0.9 maximum_select_fusion.1
  74.4 0.7 collective-permute-start.4
  75.1 0.9 fusion.17
  75.9 4.1 %collective-permute-done.4 = f32[5,1,32,128]{3,2,0,1:T(8,128)S(1)} collective-permute-done((f32[5,1,32,128]{3,2,0,1:T(8,128)S(1)}, f32[5,1,32,128]{3,2,0,1:T(8,128)S(1)}, u32[]{:S(2)}, u32[]{:S(2)}) %collective-permute-start.4) | collective-permute-done | bytes 81952 | tf_op jit(solution)/shard_map/ppermute | solution.py:92
  80.1 1.4 pad_maximum_fusion.13
  81.6 2.0 %collective-permute-start.5 = (f32[2,5,3,1,10,128]{5,3,1,4,2,0:T(1,128)S(1)}, f32[2,5,3,1,10,128]{5,3,1,4,2,0:T(1,128)S(1)}, u32[]{:S(2)}, u32[]{:S(2)}) collective-permute-start(f32[2,5,3,1,10,128]{5,3,1,4,2,0:T(1,128)S(1)} %get-tuple-element.25), channel_id=1, source_target_pairs={{0,1},{1,2},{2,3},{3,0},{4,5},{5,6},{6,7},{7,4},{8,9},{9,10},{10,1... | collective-permute-start | bytes 460808 | tf_op jit(solution)/shard_map/ppermute | solution.py:15
  83.6 0.9 slice_bitcast_fusion.5
  84.5 1.0 multiply_reduce_fusion.3
  85.5 1.0 fusion.16
  86.5 1.0 fusion.15
  87.7 0.7 collective-permute-done.2
  88.4 1.9 %collective-permute-done.5 = f32[2,5,3,1,10,128]{5,3,1,4,2,0:T(1,128)S(1)} collective-permute-done((f32[2,5,3,1,10,128]{5,3,1,4,2,0:T(1,128)S(1)}, f32[2,5,3,1,10,128]{5,3,1,4,2,0:T(1,128)S(1)}, u32[]{:S(2)}, u32[]{:S(2)}) %collective-permute-start.5) | collective-permute-done | bytes 153632 | tf_op jit(solution)/shard_map/ppermute | solution.py:15
  90.8 0.3 fusion.5
  91.1 1.7 %fusion.9 = f32[5,3,16,8,128]{4,3,2,1,0:T(8,128)S(1)} fusion(f32[5,3,16,8,128]{4,2,0,3,1:T(8,128)S(1)} %fusion.5, f32[5,3,16,8,128]{4,3,2,1,0:T(8,128)S(1)} %copy-done.2, f32[5,3,16,8,128]{4,2,0,3,1:T(8,128)S(1)} %fusion.7, f32[5,128,128]{2,1,0:T(8,128)S(1)} %copy-done.10), kind=kOutput, calls=%fused_computation.24 | convolution fusion | flops 378224640 | bytes 4259840 | tf_op jit(solution)/shard_map/slm,skyxl->skyxm/dot_general | solution.py:75
  93.0 1.1 copy-done.9
  94.3 0.7 slice.171
  95.0 1.4 slice_bitcast_fusion
  96.5 17.3 %psum.30 = f32[5,1,8,128]{3,2,0,1:T(8,128)S(1)} all-reduce(f32[5,1,8,128]{3,2,0,1:T(8,128)S(1)} %bitcast.180), channel_id=1, replica_groups=mesh['tx'=8,'ty'=4] {'ty'}, use_global_device_ids=true, to_apply=%region_13.14 | all-reduce | flops 5120 | bytes 40960 | tf_op jit(solution)/shard_map/psum | solution.py:25
  113.8 0.8 fusion.19
  114.6 22.7 %psum.31 = f32[5,1,16,128]{3,2,0,1:T(8,128)S(1)} all-reduce(f32[5,1,16,128]{3,2,0,1:T(8,128)S(1)} %fusion.19), channel_id=1, replica_groups=mesh['tx'=8,'ty'=4] {'tx'}, use_global_device_ids=true, to_apply=%region_16.17 | all-reduce | flops 10240 | bytes 81920 | tf_op jit(solution)/shard_map/psum | solution.py:25
  137.3 9.4 %all_gather.7 = f32[5,1,64,128]{3,2,0,1:T(8,128)S(1)} all-gather(f32[5,1,8,128]{3,2,0,1:T(8,128)S(1)} %psum.30), channel_id=1, replica_groups=mesh['tx'=8,'ty'=4] {'tx'}, dimensions={2}, use_global_device_ids=true | all-gather | bytes 184320 | tf_op jit(solution)/shard_map/all_gather | solution.py:87
  146.7 0.4 collective-permute-start.7
  147.1 2.3 %collective-permute-start.6 = (f32[2,5,3,16,1,128]{5,3,2,1,4,0:T(8,128)S(1)}, f32[2,5,3,16,1,128]{5,3,2,1,4,0:T(8,128)S(1)}, u32[]{:S(2)}, u32[]{:S(2)}) collective-permute-start(f32[2,5,3,16,1,128]{5,3,2,1,4,0:T(8,128)S(1)} %get-tuple-element.29), channel_id=1, source_target_pairs={{4,0},{8,4},{12,8},{16,12},{20,16},{24,20},{28,24},{0,28},{5,1},{9... | collective-permute-start | bytes 737288 | tf_op jit(solution)/shard_map/ppermute | solution.py:18
  149.4 1.5 copy.356
  151.0 0.8 collective-permute-start.10
  151.8 4.5 %collective-permute-done.10 = f32[5,1,32,128]{3,2,0,1:T(8,128)S(1)} collective-permute-done((f32[5,1,32,128]{3,2,0,1:T(8,128)S(1)}, f32[5,1,32,128]{3,2,0,1:T(8,128)S(1)}, u32[]{:S(2)}, u32[]{:S(2)}) %collective-permute-start.10) | collective-permute-done | bytes 81952 | tf_op jit(solution)/shard_map/ppermute | solution.py:92
  157.0 2.6 %collective-permute-start.8 = (f32[2,5,3,1,10,128]{5,3,2,1,4,0:T(1,128)S(1)}, f32[2,5,3,1,10,128]{5,3,2,1,4,0:T(1,128)S(1)}, u32[]{:S(2)}, u32[]{:S(2)}) collective-permute-start(f32[2,5,3,1,10,128]{5,3,2,1,4,0:T(1,128)S(1)} %get-tuple-element.22), channel_id=1, source_target_pairs={{1,0},{2,1},{3,2},{0,3},{5,4},{6,5},{7,6},{4,7},{9,8},{10,9},{11,1... | collective-permute-start | bytes 460808 | tf_op jit(solution)/shard_map/ppermute | solution.py:18
  159.9 3.0 %collective-permute-done.8 = f32[2,5,3,1,10,128]{5,3,2,1,4,0:T(1,128)S(1)} collective-permute-done((f32[2,5,3,1,10,128]{5,3,2,1,4,0:T(1,128)S(1)}, f32[2,5,3,1,10,128]{5,3,2,1,4,0:T(1,128)S(1)}, u32[]{:S(2)}, u32[]{:S(2)}) %collective-permute-start.8) | collective-permute-done | bytes 153632 | tf_op jit(solution)/shard_map/ppermute | solution.py:18
  162.9 3.8 %collective-permute-done.11 = f32[2,5,3,1,10,128]{5,3,2,1,4,0:T(1,128)S(1)} collective-permute-done((f32[2,5,3,1,10,128]{5,3,2,1,4,0:T(1,128)S(1)}, f32[2,5,3,1,10,128]{5,3,2,1,4,0:T(1,128)S(1)}, u32[]{:S(2)}, u32[]{:S(2)}) %collective-permute-start.11) | collective-permute-done | bytes 153632 | tf_op jit(solution)/shard_map/ppermute | solution.py:15
  166.9 0.4 fusion
  167.3 1.8 %fusion.4 = f32[5,3,16,8,128]{4,3,2,1,0:T(8,128)} fusion(f32[5,3,16,8,128]{4,3,2,1,0:T(8,128)S(1)} %copy-done.4, f32[5,3,16,8,128]{4,3,2,1,0:T(8,128)S(1)} %bitcast.162, f32[5,3,16,1,128]{4,3,2,1,0:T(1,128)S(1)} %copy.279, f32[5,3,16,1,128]{4,3,2,1,0:T(1,128)S(1)} %broadcast_select_fusion, f32[5,3,16,8,128]{4,2,1,0,3:T(8,128)S(1)} %fusion), kind=kLoop, calls=%fused_computation.8 | loop fusion | flops 1720320 | bytes 4177920 | tf_op jit(solution)/shard_map/add | solution.py:115
  (84 shorter events, 2.8 us)
Async XLA Ops:
  0.0 3.8 %copy-start = (f32[5,3,16,8,128]{4,3,2,1,0:T(8,128)S(1)}, f32[5,3,16,8,128]{4,3,2,1,0:T(8,128)}, u32[]{:S(2)}) copy-start(f32[5,3,16,8,128]{4,3,2,1,0:T(8,128)} %param.4) | copy-start | bytes 2949124
  5.8 1.0 copy-start.1
  6.9 31.9 %copy-start.12 = (s32[40,4]{0,1:T(4,128)S(1)}, s32[40,4]{0,1:T(4,128)}, u32[]{:S(2)}) copy-start(s32[40,4]{0,1:T(4,128)} %param.7) | copy-start | bytes 1924
  33.7 39.8 %collective-permute-start.3 = (f32[5,1,16,128]{3,2,0,1:T(8,128)S(1)}, f32[5,1,16,128]{3,2,0,1:T(8,128)}, u32[]{:S(2)}, u32[]{:S(2)}) collective-permute-start(f32[5,1,16,128]{3,2,0,1:T(8,128)S(1)} %psum.29), channel_id=1, source_target_pairs={{0,1},{1,0},{2,3},{3,2},{4,5},{5,4},{6,7},{7,6},{8,9},{9,8},{10,11... | collective-permute-start | bytes 122888 | tf_op jit(solution)/shard_map/ppermute | solution.py:92
  36.1 44.0 %collective-permute-start.1 = (f32[2,5,3,16,1,128]{5,3,1,4,2,0:T(8,128)}, f32[2,5,3,16,1,128]{5,3,1,4,2,0:T(8,128)}, u32[]{:S(2)}, u32[]{:S(2)}) collective-permute-start(f32[2,5,3,16,1,128]{5,3,1,4,2,0:T(8,128)} %get-tuple-element.32), channel_id=1, source_target_pairs={{0,4},{4,8},{8,12},{12,16},{16,20},{20,24},{24,28},{28,0},{1,5},{5... | collective-permute-start | bytes 737288 | tf_op jit(solution)/shard_map/ppermute | solution.py:15
  36.1 44.0 %collective-permute-start = (f32[2,5,3,16,1,128]{5,3,1,4,2,0:T(8,128)}, f32[2,5,3,16,1,128]{5,3,1,4,2,0:T(8,128)}, u32[]{:S(2)}, u32[]{:S(2)}) collective-permute-start(f32[2,5,3,16,1,128]{5,3,1,4,2,0:T(8,128)} %get-tuple-element.33), channel_id=1, source_target_pairs={{4,0},{8,4},{12,8},{16,12},{20,16},{24,20},{28,24},{0,28},{5,1},{9... | collective-permute-start | bytes 737288 | tf_op jit(solution)/shard_map/ppermute | solution.py:18
  40.7 32.0 %copy-start.8 = (f32[2,3,16,8,128]{4,3,2,1,0:T(8,128)S(1)}, f32[2,3,16,8,128]{4,3,2,1,0:T(8,128)}, u32[]{:S(2)}) copy-start(f32[2,3,16,8,128]{4,3,2,1,0:T(8,128)} %param.5) | copy-start | bytes 1179652
  73.5 17.1 %copy-start.13 = (f32[3]{0:T(128)}, f32[3]{0:T(128)S(1)}, u32[]{:S(2)}) copy-start(f32[3]{0:T(128)S(1)} %neg.19) | copy-start | bytes 40
  74.4 11.2 %copy-start.11 = (f32[5,16,128]{2,1,0:T(8,128)S(1)}, f32[5,16,128]{2,1,0:T(8,128)}, u32[]{:S(2)}) copy-start(f32[5,16,128]{2,1,0:T(8,128)} %dynamic-slice_bitcast_fusion.1) | copy-start | bytes 122884
  74.4 5.7 %collective-permute-start.4 = (f32[5,1,32,128]{3,2,0,1:T(8,128)S(1)}, f32[5,1,32,128]{3,2,0,1:T(8,128)S(1)}, u32[]{:S(2)}, u32[]{:S(2)}) collective-permute-start(f32[5,1,32,128]{3,2,0,1:T(8,128)S(1)} %maximum_select_fusion.1), channel_id=1, source_target_pairs={{0,2},{1,3},{2,0},{3,1},{4,6},{5,7},{6,4},{7,5},{8,10},{9,11},{10,... | collective-permute-start | bytes 245768 | tf_op jit(solution)/shard_map/ppermute | solution.py:92
  80.1 7.5 %copy-start.6 = (f32[5,3,16,8,128]{4,2,0,3,1:T(8,128)S(1)}, f32[5,3,16,8,128]{4,2,0,3,1:T(8,128)}, u32[]{:S(2)}) copy-start(f32[5,3,16,8,128]{4,2,0,3,1:T(8,128)} %get-tuple-element.30) | copy-start | bytes 2949124
  81.5 6.9 %collective-permute-start.2 = (f32[2,5,3,1,10,128]{5,3,1,4,2,0:T(1,128)S(1)}, f32[2,5,3,1,10,128]{5,3,1,4,2,0:T(1,128)S(1)}, u32[]{:S(2)}, u32[]{:S(2)}) collective-permute-start(f32[2,5,3,1,10,128]{5,3,1,4,2,0:T(1,128)S(1)} %get-tuple-element.24), channel_id=1, source_target_pairs={{1,0},{2,1},{3,2},{0,3},{5,4},{6,5},{7,6},{4,7},{9,8},{10,9},{11,1... | collective-permute-start | bytes 460808 | tf_op jit(solution)/shard_map/ppermute | solution.py:18
  81.6 8.8 %collective-permute-start.5 = (f32[2,5,3,1,10,128]{5,3,1,4,2,0:T(1,128)S(1)}, f32[2,5,3,1,10,128]{5,3,1,4,2,0:T(1,128)S(1)}, u32[]{:S(2)}, u32[]{:S(2)}) collective-permute-start(f32[2,5,3,1,10,128]{5,3,1,4,2,0:T(1,128)S(1)} %get-tuple-element.25), channel_id=1, source_target_pairs={{0,1},{1,2},{2,3},{3,0},{4,5},{5,6},{6,7},{7,4},{8,9},{9,10},{10,1... | collective-permute-start | bytes 460808 | tf_op jit(solution)/shard_map/ppermute | solution.py:15
  86.5 4.2 %copy-start.5 = (f32[5,3,16,8,128]{4,2,0,3,1:T(8,128)S(1)}, f32[5,3,16,8,128]{4,2,0,3,1:T(8,128)}, u32[]{:S(2)}) copy-start(f32[5,3,16,8,128]{4,2,0,3,1:T(8,128)} %get-tuple-element.31) | copy-start | bytes 2949124
  87.7 3.4 %copy-start.2 = (f32[5,3,16,8,128]{4,3,2,1,0:T(8,128)S(1)}, f32[5,3,16,8,128]{4,3,2,1,0:T(8,128)}, u32[]{:S(2)}) copy-start(f32[5,3,16,8,128]{4,3,2,1,0:T(8,128)} %copy-done.1) | copy-start | bytes 2949124
  87.7 3.4 %copy-start.10 = (f32[5,128,128]{2,1,0:T(8,128)S(1)}, f32[5,128,128]{2,1,0:T(8,128)}, u32[]{:S(2)}) copy-start(f32[5,128,128]{2,1,0:T(8,128)} %param.6) | copy-start | bytes 983044
  92.8 1.5 copy-start.3
  92.8 1.3 copy-start.9
  137.3 13.7 %collective-permute-start.9 = (f32[5,1,16,128]{3,2,0,1:T(8,128)S(1)}, f32[5,1,16,128]{3,2,0,1:T(8,128)S(1)}, u32[]{:S(2)}, u32[]{:S(2)}) collective-permute-start(f32[5,1,16,128]{3,2,0,1:T(8,128)S(1)} %psum.31), channel_id=1, source_target_pairs={{0,1},{1,0},{2,3},{3,2},{4,5},{5,4},{6,7},{7,6},{8,9},{9,8},{10,11... | collective-permute-start | bytes 122888 | tf_op jit(solution)/shard_map/ppermute | solution.py:92
  146.7 9.7 %collective-permute-start.7 = (f32[2,5,3,16,1,128]{5,3,1,2,4,0:T(8,128)S(1)}, f32[2,5,3,16,1,128]{5,3,1,2,4,0:T(8,128)S(1)}, u32[]{:S(2)}, u32[]{:S(2)}) collective-permute-start(f32[2,5,3,16,1,128]{5,3,1,2,4,0:T(8,128)S(1)} %copy.298), channel_id=1, source_target_pairs={{0,4},{4,8},{8,12},{12,16},{16,20},{20,24},{24,28},{28,0},{1,5},{5... | collective-permute-start | bytes 737288 | tf_op jit(solution)/shard_map/ppermute | solution.py:15
  147.1 9.3 %collective-permute-start.6 = (f32[2,5,3,16,1,128]{5,3,2,1,4,0:T(8,128)S(1)}, f32[2,5,3,16,1,128]{5,3,2,1,4,0:T(8,128)S(1)}, u32[]{:S(2)}, u32[]{:S(2)}) collective-permute-start(f32[2,5,3,16,1,128]{5,3,2,1,4,0:T(8,128)S(1)} %get-tuple-element.29), channel_id=1, source_target_pairs={{4,0},{8,4},{12,8},{16,12},{20,16},{24,20},{28,24},{0,28},{5,1},{9... | collective-permute-start | bytes 737288 | tf_op jit(solution)/shard_map/ppermute | solution.py:18
  151.0 5.4 %collective-permute-start.10 = (f32[5,1,32,128]{3,2,0,1:T(8,128)S(1)}, f32[5,1,32,128]{3,2,0,1:T(8,128)S(1)}, u32[]{:S(2)}, u32[]{:S(2)}) collective-permute-start(f32[5,1,32,128]{3,2,0,1:T(8,128)S(1)} %maximum_select_fusion.3), channel_id=1, source_target_pairs={{0,2},{1,3},{2,0},{3,1},{4,6},{5,7},{6,4},{7,5},{8,10},{9,11},{10,... | collective-permute-start | bytes 245768 | tf_op jit(solution)/shard_map/ppermute | solution.py:92
  156.7 10.2 %copy-start.7 = (f32[5,3,16,8,128]{4,2,1,0,3:T(8,128)S(1)}, f32[5,3,16,8,128]{4,2,1,0,3:T(8,128)}, u32[]{:S(2)}) copy-start(f32[5,3,16,8,128]{4,2,1,0,3:T(8,128)} %get-tuple-element.26) | copy-start | bytes 2949124
  156.7 10.2 %copy-start.14 = (f32[3]{0:T(128)S(1)}, f32[3]{0:T(128)}, u32[]{:S(2)}) copy-start(f32[3]{0:T(128)} %copy-done.13) | copy-start | bytes 40
  157.0 10.3 %copy-start.4 = (f32[5,3,16,8,128]{4,3,2,1,0:T(8,128)S(1)}, f32[5,3,16,8,128]{4,3,2,1,0:T(8,128)}, u32[]{:S(2)}) copy-start(f32[5,3,16,8,128]{4,3,2,1,0:T(8,128)} %copy-done.3) | copy-start | bytes 2949124
  157.0 5.9 %collective-permute-start.8 = (f32[2,5,3,1,10,128]{5,3,2,1,4,0:T(1,128)S(1)}, f32[2,5,3,1,10,128]{5,3,2,1,4,0:T(1,128)S(1)}, u32[]{:S(2)}, u32[]{:S(2)}) collective-permute-start(f32[2,5,3,1,10,128]{5,3,2,1,4,0:T(1,128)S(1)} %get-tuple-element.22), channel_id=1, source_target_pairs={{1,0},{2,1},{3,2},{0,3},{5,4},{6,5},{7,6},{4,7},{9,8},{10,9},{11,1... | collective-permute-start | bytes 460808 | tf_op jit(solution)/shard_map/ppermute | solution.py:18
  159.6 7.1 %collective-permute-start.11 = (f32[2,5,3,1,10,128]{5,3,2,1,4,0:T(1,128)S(1)}, f32[2,5,3,1,10,128]{5,3,2,1,4,0:T(1,128)S(1)}, u32[]{:S(2)}, u32[]{:S(2)}) collective-permute-start(f32[2,5,3,1,10,128]{5,3,2,1,4,0:T(1,128)S(1)} %get-tuple-element.23), channel_id=1, source_target_pairs={{0,1},{1,2},{2,3},{3,0},{4,5},{5,6},{6,7},{7,4},{8,9},{9,10},{10,1... | collective-permute-start | bytes 460808 | tf_op jit(solution)/shard_map/ppermute | solution.py:15
